TPU v7x, 128 devices: a whole 4x4x4 slice. The times are simulated.
128 devices in a mesh: row: 32 (over y, z, core), col: 4 (over x).
Axes of the slice: x: 4, y: 4, z: 4, core: 2. Of those that a mesh axis runs over, the one named last changes fastest.
Arguments:
- factor: float32 [4, 4096, 52, 512], P(None, 'row', None, 'col'), may hold values from -0.0390625 to 0.0390625
- earlier: float32 [20, 512, 256], P(None, 'col'), may hold values from -6 to 6
- rhs: float32 [4, 4096, 256], P(None, 'row'), may hold values from -6 to 6
- inverse: float32 [4, 4096, 4096], P(None, 'row'), may hold values from -1.4 to 1.4, as said below
Outputs:
- solution: float32 [4, 4096, 256], P(None, 'row')
Inputs may be any that keep to these rules, and one draw needn't show every extreme that they name: Each [4096, 4096] block of inverse is lower triangular, with diagonal entries from 0.6 to 1.4.
All inputs are finite; a program needn't handle non-finite values.
Results may differ from a plain program's by a relative error of at most 0.0001.
Values sent between devices are 32-bit elements; how exact they have to be, the bound alone decides.
A program may use at most 128 MiB of HBM per device.

v0:
```python
import jax
import jax.numpy as jnp
from jax import lax
from jax.sharding import PartitionSpec as P


def per_device(factor, earlier, rhs, inverse):
    steps_total = rhs.shape[0]
    tile_rows = rhs.shape[1]
    rhs_width = rhs.shape[2]
    block_rows = inverse.shape[2]
    known_groups = earlier.shape[0]
    col_count = lax.axis_size("col")
    col_pos = lax.axis_index("col")
    block_groups = block_rows // (col_count * tile_rows)
    known_terms = jnp.einsum(
        "snbk,bkm->snm",
        factor[:, :, :known_groups, :],
        earlier,
        precision=lax.Precision.HIGHEST,
        preferred_element_type=jnp.float32,
    )
    pending = [known_terms[index] for index in range(steps_total)]
    solved_tiles = []
    for step in range(steps_total):
        row_total = lax.psum(pending[step], "col")
        residual = lax.all_gather(rhs[step] - row_total, "row", axis=0, tiled=True)
        solved = jnp.dot(
            inverse[step],
            residual,
            precision=lax.Precision.HIGHEST,
            preferred_element_type=jnp.float32,
        )
        solved_tiles.append(solved)
        if step + 1 < steps_total:
            all_solved = lax.all_gather(solved, "row", axis=0, tiled=True)
            needed = lax.dynamic_index_in_dim(
                all_solved.reshape(block_groups, col_count, tile_rows, rhs_width),
                col_pos,
                1,
                keepdims=False,
            )
            first_group = known_groups + step * block_groups
            later_cols = factor[step + 1 :, :, first_group : first_group + block_groups, :]
            update = jnp.einsum(
                "snbk,bkm->snm",
                later_cols,
                needed,
                precision=lax.Precision.HIGHEST,
                preferred_element_type=jnp.float32,
            )
            for later_step in range(step + 1, steps_total):
                pending[later_step] = pending[later_step] + update[later_step - step - 1]
    return jnp.stack(solved_tiles, 0)


def solution(mesh):
    return jax.shard_map(
        per_device,
        mesh=mesh,
        in_specs=(
            P(None, "row", None, "col"),
            P(None, "col", None),
            P(None, "row", None),
            P(None, "row", None),
        ),
        out_specs=P(None, "row", None),
        check_vma=False,
    )
```

profile of v0, /device:TPU:19, one launch (start us, length us, event | category | flops | bytes accessed | tf_op | source)
XLA Modules:
  0.0 608.8 jit_solution(14477323054801304347)
XLA Ops:
  6.5 1.7 copy-done
  8.3 6.4 %fusion.16 = f32[4,128,256]{2,1,0:T(8,128)S(1)} fusion(f32[4,128,52,128]{3,1,2,0:T(8,128)} %param.4, f32[20,128,256]{2,1,0:T(8,128)S(1)} %copy-done), kind=kOutput, calls=%fused_computation.16 | convolution fusion | flops 4026531840 | bytes 16777216 | tf_op jit(solution)/shard_map/snbk,bkm->snm/dot_general | solution.py:16
  15.4 40.5 %all-reduce.5.cloned.1.call-done = f32[128,256]{1,0:T(8,128)} async-done(((f32[128,256]{1,0:T(8,128)}), f32[128,256]{1,0:T(8,128)}) %all-reduce.5.cloned.1.call-update) | async-done | bytes 131088 | tf_op jit(solution)/shard_map/psum | solution.py:26
  55.9 1.6 bitcast_subtract_fusion.3
  57.6 50.0 %all-gather.8.cloned.1.call-done = f32[4096,256]{1,0:T(8,128)} async-done(((f32[128,256]{1,0:T(8,128)}), f32[4096,256]{1,0:T(8,128)}) %all-gather.8.cloned.1.call-update) | async-done | bytes 4194320 | tf_op jit(solution)/shard_map/all_gather | solution.py:27
  107.6 10.2 %fusion.8 = f32[256,128]{1,0:T(8,128)} fusion(f32[4096,256]{1,0:T(8,128)} %all-gather.8.cloned.1.call-done, f32[4,128,4096]{2,1,0:T(8,128)} %param.7), kind=kOutput, calls=%fused_computation.8 | convolution fusion | flops 1610612736 | bytes 6422528 | tf_op jit(solution)/shard_map/dot_general | solution.py:28
  118.1 48.2 %all-gather.10.cloned.1.call-done = f32[4096,256]{0,1:T(8,128)} async-done(((f32[128,256]{0,1:T(8,128)}), f32[4096,256]{0,1:T(8,128)}) %all-gather.10.cloned.1.call-update) | async-done | bytes 4194320 | tf_op jit(solution)/shard_map/all_gather | solution.py:36
  166.2 6.1 %reshape.19 = f32[8,4,128,256]{2,1,0,3:T(4,128)} reshape(f32[4096,256]{0,1:T(8,128)} %all-gather.10.cloned.1.call-done) | data formatting | bytes 8388608 | tf_op jit(solution)/shard_map/reshape | solution.py:38
  172.4 3.3 constant_dynamic-slice_fusion.2
  175.7 2.9 fusion.19
  179.3 38.7 %all-reduce.7.cloned.1.call-done = f32[128,256]{1,0:T(8,128)} async-done(((f32[128,256]{1,0:T(8,128)}), f32[128,256]{1,0:T(8,128)}) %all-reduce.7.cloned.1.call-update) | async-done | bytes 131088 | tf_op jit(solution)/shard_map/psum | solution.py:26
  218.0 1.6 bitcast_subtract_fusion.2
  219.6 49.7 %all-gather.12.cloned.1.call-done = f32[4096,256]{1,0:T(8,128)} async-done(((f32[128,256]{1,0:T(8,128)}), f32[4096,256]{1,0:T(8,128)}) %all-gather.12.cloned.1.call-update) | async-done | bytes 4194320 | tf_op jit(solution)/shard_map/all_gather | solution.py:27
  269.3 10.2 %fusion.6 = f32[256,128]{1,0:T(8,128)} fusion(f32[4096,256]{1,0:T(8,128)} %all-gather.12.cloned.1.call-done, f32[4,128,4096]{2,1,0:T(8,128)} %param.7), kind=kOutput, calls=%fused_computation.6 | convolution fusion | flops 1610612736 | bytes 6422528 | tf_op jit(solution)/shard_map/dot_general | solution.py:28
  279.8 48.1 %all-gather.14.cloned.1.call-done = f32[4096,256]{0,1:T(8,128)} async-done(((f32[128,256]{0,1:T(8,128)}), f32[4096,256]{0,1:T(8,128)}) %all-gather.14.cloned.1.call-update) | async-done | bytes 4194320 | tf_op jit(solution)/shard_map/all_gather | solution.py:36
  327.9 6.1 %reshape.20 = f32[8,4,128,256]{2,1,0,3:T(4,128)} reshape(f32[4096,256]{0,1:T(8,128)} %all-gather.14.cloned.1.call-done) | data formatting | bytes 8388608 | tf_op jit(solution)/shard_map/reshape | solution.py:38
  334.1 3.3 constant_dynamic-slice_fusion.1
  337.3 2.3 convolution_bitcast_fusion
  339.6 0.7 fusion.35
  340.4 38.7 %all-reduce.9.cloned.1.call-done = f32[128,256]{1,0:T(8,128)} async-done(((f32[128,256]{1,0:T(8,128)}), f32[128,256]{1,0:T(8,128)}) %all-reduce.9.cloned.1.call-update) | async-done | bytes 131088 | tf_op jit(solution)/shard_map/psum | solution.py:26
  379.1 1.6 bitcast_subtract_fusion.1
  380.7 50.1 %all-gather.16.cloned.1.call-done = f32[4096,256]{1,0:T(8,128)} async-done(((f32[128,256]{1,0:T(8,128)}), f32[4096,256]{1,0:T(8,128)}) %all-gather.16.cloned.1.call-update) | async-done | bytes 4194320 | tf_op jit(solution)/shard_map/all_gather | solution.py:27
  430.8 10.2 %fusion.4 = f32[256,128]{1,0:T(8,128)} fusion(f32[4096,256]{1,0:T(8,128)} %all-gather.16.cloned.1.call-done, f32[4,128,4096]{2,1,0:T(8,128)} %param.7), kind=kOutput, calls=%fused_computation.4 | convolution fusion | flops 1610612736 | bytes 6422528 | tf_op jit(solution)/shard_map/dot_general | solution.py:28
  441.3 48.1 %all-gather.18.cloned.1.call-done = f32[4096,256]{0,1:T(8,128)} async-done(((f32[128,256]{0,1:T(8,128)}), f32[4096,256]{0,1:T(8,128)}) %all-gather.18.cloned.1.call-update) | async-done | bytes 4194320 | tf_op jit(solution)/shard_map/all_gather | solution.py:36
  489.4 6.1 %reshape.21 = f32[8,4,128,256]{2,1,0,3:T(4,128)} reshape(f32[4096,256]{0,1:T(8,128)} %all-gather.18.cloned.1.call-done) | data formatting | bytes 8388608 | tf_op jit(solution)/shard_map/reshape | solution.py:38
  495.5 3.3 constant_dynamic-slice_fusion
  498.9 2.9 fusion.25
  501.8 38.7 %all-reduce.11.cloned.1.call-done = f32[128,256]{1,0:T(8,128)} async-done(((f32[128,256]{1,0:T(8,128)}), f32[128,256]{1,0:T(8,128)}) %all-reduce.11.cloned.1.call-update) | async-done | bytes 131088 | tf_op jit(solution)/shard_map/psum | solution.py:26
  540.5 1.6 bitcast_subtract_fusion
  542.1 49.9 %all-gather.20.cloned.1.call-done = f32[4096,256]{1,0:T(8,128)} async-done(((f32[128,256]{1,0:T(8,128)}), f32[4096,256]{1,0:T(8,128)}) %all-gather.20.cloned.1.call-update) | async-done | bytes 4194320 | tf_op jit(solution)/shard_map/all_gather | solution.py:27
  592.0 9.2 %fusion.22 = f32[1,128,256]{1,2,0:T(8,128)S(1)} fusion(f32[4096,256]{1,0:T(8,128)} %all-gather.20.cloned.1.call-done, f32[4,128,4096]{2,1,0:T(8,128)} %param.7), kind=kOutput, calls=%fused_computation.19 | convolution fusion | flops 1610612736 | bytes 6422528 | tf_op jit(solution)/shard_map/dot_general | solution.py:28
  601.3 1.0 copy.9
  (36 shorter events, 2.7 us)
Async XLA Ops:
  6.5 1.7 copy-start
  6.5 49.4 %all-reduce.5.cloned.1.call-start = ((), (), s32[]{:S(2)}) async-start(), calls=%async_computation | async-start | bytes 262144 | tf_op jit(solution)/shard_map/psum | solution.py:26
  15.4 92.2 %all-gather.8.cloned.1.call-start = ((), (), s32[]{:S(2)}) async-start(), calls=%async_computation.1 | async-start | bytes 4325376 | tf_op jit(solution)/shard_map/all_gather | solution.py:27
  57.6 108.7 %all-gather.10.cloned.1.call-start = ((), (), s32[]{:S(2)}) async-start(), calls=%async_computation.2 | async-start | bytes 4325376 | tf_op jit(solution)/shard_map/all_gather | solution.py:36
  117.8 100.2 %all-reduce.7.cloned.1.call-start = ((), (), s32[]{:S(2)}) async-start(), calls=%async_computation.3 | async-start | bytes 262144 | tf_op jit(solution)/shard_map/psum | solution.py:26
  172.4 45.6 %copy-start.5 = (f32[4,128,256]{2,1,0:T(8,128)S(1)}, f32[4,128,256]{2,1,0:T(8,128)}, u32[]{:S(2)}) copy-start(f32[4,128,256]{2,1,0:T(8,128)} %param.6) | copy-start | bytes 1572868
  179.3 90.1 %all-gather.12.cloned.1.call-start = ((), (), s32[]{:S(2)}) async-start(), calls=%async_computation.4 | async-start | bytes 4325376 | tf_op jit(solution)/shard_map/all_gather | solution.py:27
  219.6 108.3 %all-gather.14.cloned.1.call-start = ((), (), s32[]{:S(2)}) async-start(), calls=%async_computation.5 | async-start | bytes 4325376 | tf_op jit(solution)/shard_map/all_gather | solution.py:36
  279.5 99.6 %all-reduce.9.cloned.1.call-start = ((), (), s32[]{:S(2)}) async-start(), calls=%async_computation.6 | async-start | bytes 262144 | tf_op jit(solution)/shard_map/psum | solution.py:26
  340.3 90.5 %all-gather.16.cloned.1.call-start = ((), (), s32[]{:S(2)}) async-start(), calls=%async_computation.7 | async-start | bytes 4325376 | tf_op jit(solution)/shard_map/all_gather | solution.py:27
  380.7 108.8 %all-gather.18.cloned.1.call-start = ((), (), s32[]{:S(2)}) async-start(), calls=%async_computation.8 | async-start | bytes 4325376 | tf_op jit(solution)/shard_map/all_gather | solution.py:36
  441.0 99.5 %all-reduce.11.cloned.1.call-start = ((), (), s32[]{:S(2)}) async-start(), calls=%async_computation.9 | async-start | bytes 262144 | tf_op jit(solution)/shard_map/psum | solution.py:26
  498.8 102.4 %copy-start.2 = (f32[256,128]{1,0:T(8,128)S(1)}, f32[256,128]{1,0:T(8,128)}, u32[]{:S(2)}) copy-start(f32[256,128]{1,0:T(8,128)} %fusion.8) | copy-start | bytes 393220
  498.8 102.4 %copy-start.3 = (f32[256,128]{1,0:T(8,128)S(1)}, f32[256,128]{1,0:T(8,128)}, u32[]{:S(2)}) copy-start(f32[256,128]{1,0:T(8,128)} %fusion.6) | copy-start | bytes 393220
  498.8 102.4 %copy-start.4 = (f32[256,128]{1,0:T(8,128)S(1)}, f32[256,128]{1,0:T(8,128)}, u32[]{:S(2)}) copy-start(f32[256,128]{1,0:T(8,128)} %fusion.4) | copy-start | bytes 393220
  501.8 90.2 %all-gather.20.cloned.1.call-start = ((), (), s32[]{:S(2)}) async-start(), calls=%async_computation.10 | async-start | bytes 4325376 | tf_op jit(solution)/shard_map/all_gather | solution.py:27
  542.1 60.2 %copy-start.1 = (f32[20,128,256]{2,1,0:T(8,128)S(1)}, f32[20,128,256]{2,1,0:T(8,128)}, u32[]{:S(2)}) copy-start(f32[20,128,256]{2,1,0:T(8,128)} %param.5) | copy-start | bytes 7864324
Sparse Core Ops, SparseCore 0:
  15.5 40.3 all-reduce.4
  58.4 49.1 all-gather.7
  118.0 48.2 all-gather.9
  179.4 38.5 all-reduce.6
  220.1 49.1 all-gather.11
  279.6 48.2 all-gather.13
  340.4 38.5 all-reduce.8
  381.6 49.1 all-gather.15
  441.1 48.2 all-gather.17
  501.9 38.5 all-reduce.10
  542.8 49.1 all-gather.19
where the time goes:
time: 612 us; the launch traced here: 609 us
  waiting for transfers between devices  501 us (82%)
  matrix products  54.2 us (9%)
  local copies, waits for them, and re-layouts  31.6 us (5%)
  between operations  13.3 us (2%)
  other arithmetic  7.73 us (1%)
    all_gather x4, waiting for transfers between devices, per_device(): residual = lax.all_gather(rhs[step] - row_total, 'row', axis=0, tiled=True)  200 us
    psum x4, waiting for transfers between devices, per_device(): row_total = lax.psum(pending[step], 'col')  157 us
    all_gather x3, waiting for transfers between devices, per_device(): all_solved = lax.all_gather(solved, 'row', axis=0, tiled=True)  144 us
    dot_general x4, matrix products, per_device(): jnp.dot(inverse[step], residual, precision=lax.Precision.HIGHEST, preferr...  39.7 us
    reshape x3, local copies, waits for them, and re-layouts, per_device(): all_solved.reshape(block_groups, col_count, tile_rows, rhs_width)  18.3 us
  transfers between devices with their start and end apart: 11, of which 11 were waited for; matrix products, arithmetic and copies ran while one was open for 0% of the time, Pallas kernels for 0%

commit v1 on v0

v1 whole, which is shorter than its diff:
```python
import functools

import jax
import jax.numpy as jnp
from jax import lax
from jax.experimental import pallas as pl
from jax.experimental.pallas import tpu as pltpu
from jax.sharding import PartitionSpec as P

F32 = jnp.float32
BF16 = jnp.bfloat16
MESH = pl.DeviceIdType.MESH
STEPS = 4
KNOWN = 20
GROUPS = 8
CHAINS = 2
T = 32
PAIRS = [(1, 0), (2, 0), (2, 1), (3, 0), (3, 1), (3, 2)]
SLOT = {pair: index for index, pair in enumerate(PAIRS)}


def halves(value):
    high = value.astype(BF16)
    return high, (value - high.astype(F32)).astype(BF16)


def dot(left, right):
    return lax.dot_general(left, right, (((1,), (0,)), ((), ())), preferred_element_type=F32)


def kernel(
    factor, earlier, rhs, inverse, out,
    y_raw, y_parts, f_raw, f_parts, u_raw, u_parts, i_raw, i_parts, b_raw, b_turn,
    known, known_in, start, res, sol, upd_in, part_in, part, upd, later, done, turned, a_res, a_sol,
    ld, sib_s, sib_r, kn_s, kn_r, g1_s, g1_r, pt_s, pt_r, g2_s, g2_r, ot_s, ot_r, up_s, up_r, wr,
):
    row = lax.axis_index("row")
    x = lax.axis_index("col")
    y, z, j = row // 8, (row // 2) % 4, row % 2
    m = row // 2

    def at(x_, y_, z_, j_):
        return ((y_ * 4 + z_) * 2 + j_, x_)

    sibling = at(x, y, z, 1 - j)
    spread = x // 2
    own_zone = (z % 2) == (x // 2)
    g_here = jnp.where(own_zone, 0, 1)
    z_row = jnp.where(own_zone, z, (z + 3) % 4)
    q_here = 2 * g_here + j
    sol_slot = g_here * 8 + y * 2 + z_row // 2
    self_part = (z % 2 == 0) & (x < 2) & (j == x)
    self_out = own_zone & (x % 2 == j)
    self_upd = (x % 2) == j

    def send(src, dst, ss, rs, device):
        pltpu.make_async_remote_copy(
            src_ref=src, dst_ref=dst, send_sem=ss, recv_sem=rs, device_id=device, device_id_type=MESH
        ).start()

    def wait_recv(ref, sem):
        pltpu.make_async_remote_copy(
            src_ref=ref, dst_ref=ref, send_sem=sem, recv_sem=sem, device_id=sibling, device_id_type=MESH
        ).wait_recv()

    def wait_send(ref, sem):
        pltpu.make_async_remote_copy(
            src_ref=ref, dst_ref=ref, send_sem=sem, recv_sem=sem, device_id=sibling, device_id_type=MESH
        ).wait_send()

    def wait_local(ref, sem):
        pltpu.make_async_copy(ref, ref, sem).wait()

    def loop(lo, hi, body):
        lax.fori_loop(lo, hi, lambda index, carry: (body(index), carry)[1], 0)

    def load_known(step):
        def one(group):
            pltpu.make_async_copy(factor.at[step, :, group, :], f_raw.at[step, group], ld.at[2 + step]).start()

        loop(0, KNOWN, one)

    def load_inverse(step):
        def one(tile):
            lanes = pl.ds(pl.multiple_of((2 * tile + j) * 128, 128), 128)
            pltpu.make_async_copy(inverse.at[step, :, lanes], i_raw.at[step, j, tile], ld.at[6 + step]).start()

        loop(0, 16, one)

    def share_inverse(step):
        def one(tile):
            lanes = pl.ds(pl.multiple_of((2 * tile + 1 - j) * 128, 128), 128)
            send(inverse.at[step, :, lanes], i_raw.at[step, j, tile], sib_s.at[step], sib_r.at[step], sibling)

        loop(0, 16, one)

    def load_update(pair):
        later_step, step = pair
        slot = SLOT[pair]

        def one(group):
            pltpu.make_async_copy(
                factor.at[later_step, :, KNOWN + step * GROUPS + group, :], u_raw.at[slot, j, group], ld.at[10 + slot]
            ).start()

        loop(0, GROUPS, one)

    def share_update(pair):
        slot = SLOT[pair]
        wait_local(u_raw.at[slot, j], ld.at[10 + slot])
        send(u_raw.at[slot, j], u_raw.at[slot, j], sib_s.at[4 + slot], sib_r.at[4 + slot], sibling)

    def prepare_inverse(step):
        wait_local(i_raw.at[step, j], ld.at[6 + step])
        wait_recv(i_raw.at[step, 1 - j], sib_r.at[step])

        def one(tile):
            rows = pl.ds(pl.multiple_of(tile * 128, 128), 128)
            for t in range(2):
                high, low = halves(i_raw[step, t, tile])
                i_parts[step, rows, t * 256 : t * 256 + 128] = high.T
                i_parts[step, rows, t * 256 + 128 : t * 256 + 256] = low.T

        loop(0, 16, one)

    def prepare_update(pair):
        slot = SLOT[pair]
        wait_recv(u_raw.at[slot, 1 - j], sib_r.at[4 + slot])

        def one(group):
            rows = pl.ds(pl.multiple_of(group * 128, 128), 128)
            for t in range(2):
                high, low = halves(u_raw[slot, t, group])
                u_parts[slot, rows, t * 256 : t * 256 + 128] = high.T
                u_parts[slot, rows, t * 256 + 128 : t * 256 + 256] = low.T

        loop(0, GROUPS, one)

    def known_terms(step):
        wait_local(f_raw.at[step], ld.at[2 + step])

        def one(group):
            lanes = pl.ds(pl.multiple_of(group * 128, 128), 128)
            high, low = halves(f_raw[step, group])
            f_parts[0:128, lanes] = high
            f_parts[128:256, lanes] = low

        loop(0, KNOWN, one)
        both = dot(f_parts[...], y_parts[...])
        total = both[0:128, 0:256] + (both[0:128, 256:512] + both[128:256, 0:256] + both[128:256, 256:512])
        known[step] = -(total.T)
        b_turn[...] = b_raw[step].T
        mine = pl.ds(pl.multiple_of(x * 64, 64), 64)
        known_in[step, x] = b_turn[mine] + known[step, mine]

    def send_known(step):
        for hop in (2, 1, 3):
            q = (x + hop) % 4
            rows = pl.ds(pl.multiple_of(q * 64, 64), 64)
            send(known.at[step, rows], known_in.at[step, x], kn_s.at[step], kn_r.at[step], at(q, y, z, j))

    def collect_known(step):
        wait_recv(known_in.at[step, pl.ds(0, 3)], kn_r.at[step])
        total = known_in[step, 0] + known_in[step, 1] + known_in[step, 2] + known_in[step, 3]
        for h in range(CHAINS):
            start[step, h] = total[h * T : (h + 1) * T]

    def send_residual(step, h):
        if step == 0:
            res[step, h, m] = start[step, h]
        else:

            @pl.when(self_upd)
            def _():
                wait_recv(upd_in.at[step - 1, h, pl.ds(0, 3)], up_r.at[step - 1, h])

            @pl.when(jnp.logical_not(self_upd))
            def _():
                wait_recv(upd_in.at[step - 1, h], up_r.at[step - 1, h])

            res[step, h, m] = start[step, h] + (
                upd_in[step - 1, h, 0] + upd_in[step - 1, h, 1] + upd_in[step - 1, h, 2] + upd_in[step - 1, h, 3]
            )

        def one(other):
            send(
                res.at[step, h, m], res.at[step, h, m], g1_s.at[step, h, other], g1_r.at[step, h, m],
                at(x, other // 4, other % 4, j),
            )

        loop(m + 1, 16, one)

    def drain_residual(step, h):
        def one(other):
            wait_send(res.at[step, h, m], g1_s.at[step, h, other])

        loop(m + 1, 16, one)

    def solve(step, h):
        def place(tile):
            lanes = pl.ds(pl.multiple_of(tile * 128, 128), 128)
            high, low = halves(res[step, h, tile])
            a_res[h, 0:T, lanes] = high
            a_res[h, T : 2 * T, lanes] = low

        def arrived(tile):
            wait_recv(res.at[step, h, tile], g1_r.at[step, h, tile])
            place(tile)

        place(m)
        loop(0, m, arrived)
        both = dot(a_res[h], i_parts[step])
        for t in range(2):
            o = t * 256
            part[step, h, t] = both[0:T, o : o + 128] + (
                both[0:T, o + 128 : o + 256] + both[T : 2 * T, o : o + 128] + both[T : 2 * T, o + 128 : o + 256]
            )

        def to(t):
            send(
                part.at[step, h, t], part_in.at[step, h, j], pt_s.at[step, h, t], pt_r.at[step, h, j],
                at((z % 2) * 2 + t, y, (z + spread) % 4, x % 2),
            )

        for t in range(2):
            here = self_part & (x == t)

            @pl.when(here)
            def _():
                part_in[step, h, j] = part[step, h, t]

            @pl.when(jnp.logical_not(here))
            def _():
                to(t)

    def drain_part(step, h):
        for t in range(2):

            @pl.when(jnp.logical_not(self_part & (x == t)))
            def _():
                wait_send(part.at[step, h, t], pt_s.at[step, h, t])

    def send_solution(step, h):
        for k in range(2):

            @pl.when(jnp.logical_not(self_part & (j == k)))
            def _():
                wait_recv(part_in.at[step, h, k], pt_r.at[step, h, k])

        sol[step, h, sol_slot] = part_in[step, h, 0] + part_in[step, h, 1]
        mine = sol.at[step, h, sol_slot]
        if step + 1 < STEPS:

            def one(index):
                other = (9 + index) % 15 + 1
                send(
                    mine, mine, g2_s.at[step, h], g2_r.at[step, h],
                    at(x, (y + other // 4) % 4, (z + other % 4) % 4, j),
                )

            loop(0, 15, one)
        rows = pl.ds(pl.multiple_of(q_here * 64 + h * T, T), T)
        for hop in (2, 1, 3):
            send(mine, done.at[step, rows], ot_s.at[step, h], ot_r.at[step], at((x + hop) % 4, y, z_row, x % 2))

        @pl.when(self_out)
        def _():
            done[step, rows] = sol[step, h, sol_slot]

        @pl.when(jnp.logical_not(self_out))
        def _():
            send(mine, done.at[step, rows], ot_s.at[step, h], ot_r.at[step], at(x, y, z_row, x % 2))

    def drain_solution(step, h):
        if step + 1 < STEPS:
            wait_send(sol.at[step, h, pl.ds(0, 15)], g2_s.at[step, h])

        @pl.when(self_out)
        def _():
            wait_send(sol.at[step, h, pl.ds(0, 3)], ot_s.at[step, h])

        @pl.when(jnp.logical_not(self_out))
        def _():
            wait_send(sol.at[step, h, pl.ds(0, 4)], ot_s.at[step, h])

    def gather_solution(step, h):
        wait_recv(sol.at[step, h, pl.ds(0, 15)], g2_r.at[step, h])
        for g in range(2):
            for b in range(GROUPS):
                high, low = halves(sol[step, h, g * 8 + b])
                a_sol[h, g * T : (g + 1) * T, b * 128 : (b + 1) * 128] = high
                a_sol[h, 2 * T + g * T : 2 * T + (g + 1) * T, b * 128 : (b + 1) * 128] = low

    def update(step, later_step, h):
        both = dot(a_sol[h], u_parts[SLOT[later_step, step]])
        for t in range(2):
            o = t * 256
            total = both[0 : 2 * T, o : o + 128] + (
                both[0 : 2 * T, o + 128 : o + 256]
                + both[2 * T : 4 * T, o : o + 128]
                + both[2 * T : 4 * T, o + 128 : o + 256]
            )
            if step > 0:
                total = total + later[later_step - 2, h, t]
            if later_step > step + 1:
                later[later_step - 2, h, t] = total
            else:
                for g in range(2):
                    upd[step, h, t, g] = -total[g * T : (g + 1) * T]
        if later_step > step + 1:
            return
        for t in range(2):
            for g in range(2):
                here = (x == 2 * g + j) & (j == t)

                @pl.when(here)
                def _():
                    upd_in[step, h, x] = upd[step, h, t, g]

                @pl.when(jnp.logical_not(here))
                def _():
                    send(
                        upd.at[step, h, t, g], upd_in.at[step, h, x], up_s.at[step, h], up_r.at[step, h],
                        at(2 * g + j, y, z, t),
                    )

    def drain_update(step, h):
        @pl.when(self_upd)
        def _():
            wait_send(upd_in.at[step, h, pl.ds(0, 3)], up_s.at[step, h])

        @pl.when(jnp.logical_not(self_upd))
        def _():
            wait_send(upd_in.at[step, h], up_s.at[step, h])

    def write(step):
        @pl.when(self_out)
        def _():
            wait_recv(done.at[step, pl.ds(0, 6 * T)], ot_r.at[step])

        @pl.when(jnp.logical_not(self_out))
        def _():
            wait_recv(done.at[step], ot_r.at[step])

        turned[step] = done[step].T
        pltpu.make_async_copy(turned.at[step], out.at[step], wr.at[step]).start()

    barrier = pltpu.get_barrier_semaphore()

    def greet(device):
        pl.semaphore_signal(barrier, inc=1, device_id=device, device_id_type=MESH)

    pltpu.make_async_copy(earlier, y_raw, ld.at[0]).start()
    load_known(0)
    pltpu.make_async_copy(rhs, b_raw, ld.at[1]).start()
    load_inverse(0)

    def greet_plane(other):
        greet(at(x, (y + other // 4) % 4, (z + other % 4) % 4, j))

    loop(1, 16, greet_plane)
    for hop in range(4):
        for core in range(2):
            if (hop, core) != (0, 0):
                greet(at((x + hop) % 4, y, z, (j + core) % 2))
            greet(at((x + hop) % 4, y, (z + 1) % 4, (j + core) % 2))
            greet(at((x + hop) % 4, y, (z + 3) % 4, (j + core) % 2))
    a_res[...] = jnp.zeros_like(a_res)
    wait_local(y_raw, ld.at[0])

    def split_earlier(group):
        rows = pl.ds(pl.multiple_of(group * 128, 128), 128)
        high, low = halves(y_raw[group])
        y_parts[rows, 0:256] = high
        y_parts[rows, 256:512] = low

    loop(0, KNOWN, split_earlier)
    wait_local(b_raw, ld.at[1])
    known_terms(0)
    pl.semaphore_wait(barrier, 15 + 7 + 16)
    send_known(0)
    share_inverse(0)
    load_update(PAIRS[0])
    load_known(1)
    share_update(PAIRS[0])
    load_known(2)
    load_known(3)
    collect_known(0)
    for h in range(CHAINS):
        send_residual(0, h)
    prepare_inverse(0)
    for step in range(1, STEPS):
        load_inverse(step)
    for pair in PAIRS[1:]:
        load_update(pair)

    for step in range(STEPS):
        for h in range(CHAINS):
            solve(step, h)
        if step == 0:
            prepare_update(PAIRS[0])
            known_terms(1)
            send_known(1)
        elif step + 1 < STEPS:
            for h in range(CHAINS):
                drain_residual(step - 1, h)
                drain_solution(step - 1, h)
                drain_part(step - 1, h)
        for h in range(CHAINS):
            send_solution(step, h)
        if step + 1 == STEPS:
            break
        if step == 0:
            share_inverse(1)
            for pair in PAIRS[1:]:
                share_update(pair)
            known_terms(2)
            send_known(2)
            known_terms(3)
            send_known(3)
            collect_known(1)
            prepare_update((2, 0))
            prepare_update((3, 0))
        elif step == 1:
            share_inverse(3)
            prepare_inverse(2)
        for h in range(CHAINS):
            gather_solution(step, h)
            update(step, step + 1, h)
        for later_step in range(step + 2, STEPS):
            for h in range(CHAINS):
                update(step, later_step, h)
        if step == 0:
            share_inverse(2)
            collect_known(2)
            collect_known(3)
        for h in range(CHAINS):
            send_residual(step + 1, h)
        if step == 0:
            prepare_inverse(1)
            prepare_update((2, 1))
            prepare_update((3, 1))
        elif step == 1:
            prepare_inverse(3)
            prepare_update((3, 2))
        write(step)
        for h in range(CHAINS):
            drain_update(step, h)

    for step in range(STEPS):
        wait_send(known.at[step, pl.ds(0, 192)], kn_s.at[step])
        wait_send(i_raw.at[step, j], sib_s.at[step])
    for slot in range(len(PAIRS)):
        wait_send(u_raw.at[slot, j], sib_s.at[4 + slot])
    for step in range(STEPS - 2, STEPS):
        for h in range(CHAINS):
            drain_residual(step, h)
            drain_part(step, h)
            drain_solution(step, h)
    write(STEPS - 1)
    for step in range(STEPS):
        wait_local(turned.at[step], wr.at[step])


def per_device(factor, earlier, rhs, inverse):
    dma = pltpu.SemaphoreType.DMA
    vmem = pltpu.VMEM
    updates = len(PAIRS)
    return pl.pallas_call(
        kernel,
        out_shape=jax.ShapeDtypeStruct(rhs.shape, F32),
        in_specs=[pl.BlockSpec(memory_space=pl.ANY)] * 4,
        out_specs=pl.BlockSpec(memory_space=pl.ANY),
        scratch_shapes=[
            vmem((KNOWN, 128, 256), F32),
            vmem((KNOWN * 128, 512), BF16),
            vmem((STEPS, KNOWN, 128, 128), F32),
            vmem((256, KNOWN * 128), BF16),
            vmem((updates, 2, GROUPS, 128, 128), F32),
            vmem((updates, GROUPS * 128, 512), BF16),
            vmem((STEPS, 2, 16, 128, 128), F32),
            vmem((STEPS, 2048, 512), BF16),
            vmem((STEPS, 128, 256), F32),
            vmem((256, 128), F32),
            vmem((STEPS, 256, 128), F32),
            vmem((STEPS, 4, 64, 128), F32),
            vmem((STEPS, CHAINS, T, 128), F32),
            vmem((STEPS, CHAINS, 16, T, 128), F32),
            vmem((STEPS, CHAINS, 16, T, 128), F32),
            vmem((STEPS - 1, CHAINS, 4, T, 128), F32),
            vmem((STEPS, CHAINS, 2, T, 128), F32),
            vmem((STEPS, CHAINS, 2, T, 128), F32),
            vmem((STEPS - 1, CHAINS, 2, 2, T, 128), F32),
            vmem((2, CHAINS, 2, 2 * T, 128), F32),
            vmem((STEPS, 256, 128), F32),
            vmem((STEPS, 128, 256), F32),
            vmem((CHAINS, 2 * T, 2048), BF16),
            vmem((CHAINS, 4 * T, 1024), BF16),
            dma((16,)),
            dma((10,)),
            dma((10,)),
            dma((STEPS,)),
            dma((STEPS,)),
            dma((STEPS, CHAINS, 16)),
            dma((STEPS, CHAINS, 16)),
            dma((STEPS, CHAINS, 2)),
            dma((STEPS, CHAINS, 2)),
            dma((STEPS, CHAINS)),
            dma((STEPS, CHAINS)),
            dma((STEPS, CHAINS)),
            dma((STEPS,)),
            dma((STEPS, CHAINS)),
            dma((STEPS, CHAINS)),
            dma((STEPS,)),
        ],
        compiler_params=pltpu.CompilerParams(
            collective_id=0, has_side_effects=True, vmem_limit_bytes=60 * 1024 * 1024
        ),
        cost_estimate=pl.CostEstimate(flops=6_000_000_000, bytes_accessed=20_000_000, transcendentals=0),
        name="substitution",
    )(factor, earlier, rhs, inverse)


def solution(mesh):
    return jax.shard_map(
        per_device,
        mesh=mesh,
        in_specs=(
            P(None, "row", None, "col"),
            P(None, "col", None),
            P(None, "row", None),
            P(None, "row", None),
        ),
        out_specs=P(None, "row", None),
        check_vma=False,
    )
```

time: 612 us -> 119 us (0.19)
  waiting for transfers between devices: 501 us -> 0 us
  Pallas kernels: 0 us -> 96.9 us
  matrix products: 54.2 us -> 0 us
  between operations: 13.3 us -> 0.01 us
  local copies, waits for them, and re-layouts: 31.6 us -> 19.9 us
  other arithmetic: 7.73 us -> 0 us
    all_gather x7 -> x0, waiting for transfers between devices: 344 us -> none  [the longest x4 200 us: per_device(): residual = lax.all_gather(rhs[step] - row_total, 'row', axis=0, tiled=True)]
    psum x4 -> x0, waiting for transfers between devices: 157 us -> none  [per_device(): row_total = lax.psum(pending[step], 'col')]
    pallas_call x0 -> x1, Pallas kernels: none -> 96.9 us  [per_device(): pl.pallas_call(kernel, out_shape=jax.ShapeDtypeStruct(rhs.shape, F32), in...]
    dot_general x8 -> x0, matrix products: 54.2 us -> none  [the longest x4 39.7 us: per_device(): jnp.dot(inverse[step], residual, precision=lax.Precision.HIGHEST, preferr...]
    reshape x3 -> x0, local copies, waits for them, and re-layouts: 18.3 us -> none  [per_device(): all_solved.reshape(block_groups, col_count, tile_rows, rhs_width)]
    unnamed x12 -> x2, local copies, waits for them, and re-layouts: 1.76 us -> 19.9 us
    dynamic_slice x3 -> x0, local copies, waits for them, and re-layouts: 9.86 us -> none  [per_device(): lax.dynamic_index_in_dim(all_solved.reshape(block_groups, col_count, tile...]
    sub x4 -> x0, other arithmetic: 6.36 us -> none  [per_device(): residual = lax.all_gather(rhs[step] - row_total, 'row', axis=0, tiled=True)]
  transfers between devices with their start and end apart: 11 -> 0, of which waited for: 11 -> 0; matrix products, arithmetic and copies ran while one was open for 0% -> 0% of each run, Pallas kernels for 0% -> 0%
where the time goes in v1:
time: 119 us; the launch traced here: 117 us
  Pallas kernels  96.9 us (81%)
  local copies, waits for them, and re-layouts  19.9 us (17%)
    pallas_call x1, Pallas kernels, per_device(): pl.pallas_call(kernel, out_shape=jax.ShapeDtypeStruct(rhs.shape, F32), in...  96.9 us
    unnamed x2, local copies, waits for them, and re-layouts  19.9 us

profile of v1, /device:TPU:19, one launch (start us, length us, event | category | flops | bytes accessed | tf_op | source)
XLA Modules:
  0.0 116.8 jit_solution(7358076192888585540)
XLA Ops:
  0.0 18.0 %copy.5.factor = f32[4,128,52,128]{3,2,1,0:T(8,128)} copy(f32[4,128,52,128]{3,1,2,0:T(8,128)} %param.4) | data formatting | bytes 27262976 | tf_op args[0]
  18.0 96.9 %substitution.1 = f32[4,128,256]{2,1,0:T(8,128)} custom-call(f32[4,128,52,128]{3,2,1,0:T(8,128)} %copy.5.factor, f32[20,128,256]{2,1,0:T(8,128)} %earlier.1, f32[4,128,256]{2,1,0:T(8,128)} %rhs.1, f32[4,128,4096]{2,1,0:T(8,128)} %inverse.1), custom_call_target="tpu_custom_call" | custom-call | flops 6000000000 | bytes 20000000 | tf_op jit(solution)/shard_map/substitution/pallas_call | solution.py:469
  115.0 1.9 %copy.7 = f32[4,128,256]{2,1,0:T(8,128)} copy(f32[4,128,256]{2,1,0:T(8,128)} %substitution.1) | data formatting | bytes 1048576

commit v2 on v1

--- a/solution.py
+++ b/solution.py
@@ -75,10 +75,7 @@
         lax.fori_loop(lo, hi, lambda index, carry: (body(index), carry)[1], 0)
 
     def load_known(step):
-        def one(group):
-            pltpu.make_async_copy(factor.at[step, :, group, :], f_raw.at[step, group], ld.at[2 + step]).start()
-
-        loop(0, KNOWN, one)
+        pltpu.make_async_copy(factor.at[step, pl.ds(0, KNOWN)], f_raw.at[step], ld.at[2 + step]).start()
 
     def load_inverse(step):
         def one(tile):
@@ -97,13 +94,8 @@
     def load_update(pair):
         later_step, step = pair
         slot = SLOT[pair]
-
-        def one(group):
-            pltpu.make_async_copy(
-                factor.at[later_step, :, KNOWN + step * GROUPS + group, :], u_raw.at[slot, j, group], ld.at[10 + slot]
-            ).start()
-
-        loop(0, GROUPS, one)
+        groups = pl.ds(KNOWN + step * GROUPS, GROUPS)
+        pltpu.make_async_copy(factor.at[later_step, groups], u_raw.at[slot, j], ld.at[10 + slot]).start()
 
     def share_update(pair):
         slot = SLOT[pair]
@@ -518,7 +510,7 @@
         ),
         cost_estimate=pl.CostEstimate(flops=6_000_000_000, bytes_accessed=20_000_000, transcendentals=0),
         name="substitution",
-    )(factor, earlier, rhs, inverse)
+    )(jnp.transpose(factor, (0, 2, 1, 3)), earlier, rhs, inverse)
 
 
 def solution(mesh):

time: 119 us -> 101 us (0.85)
  local copies, waits for them, and re-layouts: 19.9 us -> 1.87 us
    unnamed x2 -> x1, local copies, waits for them, and re-layouts: 19.9 us -> 1.87 us
where the time goes in v2:
time: 101 us; the launch traced here: 98.7 us
  Pallas kernels  96.8 us (96%)
  local copies, waits for them, and re-layouts  1.87 us (2%)
    pallas_call x1, Pallas kernels, per_device(): pl.pallas_call(kernel, out_shape=jax.ShapeDtypeStruct(rhs.shape, F32), in...  96.8 us

profile of v2, /device:TPU:19, one launch (start us, length us, event | category | flops | bytes accessed | tf_op | source)
XLA Modules:
  0.0 98.7 jit_solution(14647582086682243988)
XLA Ops:
  0.0 96.8 %substitution.1 = f32[4,128,256]{2,1,0:T(8,128)} custom-call(f32[4,52,128,128]{3,2,1,0:T(8,128)} %bitcast.1, f32[20,128,256]{2,1,0:T(8,128)} %earlier.1, f32[4,128,256]{2,1,0:T(8,128)} %rhs.1, f32[4,128,4096]{2,1,0:T(8,128)} %inverse.1), custom_call_target="tpu_custom_call" | custom-call | flops 6000000000 | bytes 20000000 | tf_op jit(solution)/shard_map/substitution/pallas_call | solution.py:461
  96.8 1.9 %copy.6 = f32[4,128,256]{2,1,0:T(8,128)} copy(f32[4,128,256]{2,1,0:T(8,128)} %substitution.1) | data formatting | bytes 1048576

commit v3 on v2

--- a/solution.py
+++ b/solution.py
@@ -15,6 +15,7 @@
 GROUPS = 8
 CHAINS = 2
 T = 32
+PLANE = [(2, 2), (2, 1), (2, 3), (1, 2), (3, 2), (2, 0), (0, 2), (1, 1), (1, 3), (3, 1), (3, 3), (1, 0), (3, 0), (0, 1), (0, 3)]
 PAIRS = [(1, 0), (2, 0), (2, 1), (3, 0), (3, 1), (3, 2)]
 SLOT = {pair: index for index, pair in enumerate(PAIRS)}
 
@@ -31,8 +32,8 @@
 def kernel(
     factor, earlier, rhs, inverse, out,
     y_raw, y_parts, f_raw, f_parts, u_raw, u_parts, i_raw, i_parts, b_raw, b_turn,
-    known, known_in, start, res, sol, upd_in, part_in, part, upd, later, done, turned, a_res, a_sol,
-    ld, sib_s, sib_r, kn_s, kn_r, g1_s, g1_r, pt_s, pt_r, g2_s, g2_r, ot_s, ot_r, up_s, up_r, wr,
+    known, known_in, start, res, sol, upd_in, part_in, part, upd, later, done, turned, last_in, a_res, a_sol,
+    ld, sib_s, sib_r, kn_s, kn_r, g1_s, g1_r, pt_s, pt_r, g2_s, g2_r, ot_s, ot_r, up_s, up_r, ls_s, ls_r, wr,
 ):
     row = lax.axis_index("row")
     x = lax.axis_index("col")
@@ -43,15 +44,14 @@
         return ((y_ * 4 + z_) * 2 + j_, x_)
 
     sibling = at(x, y, z, 1 - j)
-    spread = x // 2
     own_zone = (z % 2) == (x // 2)
     g_here = jnp.where(own_zone, 0, 1)
     z_row = jnp.where(own_zone, z, (z + 3) % 4)
-    q_here = 2 * g_here + j
+    q_here = (x + 2 * j + g_here) % 4
     sol_slot = g_here * 8 + y * 2 + z_row // 2
-    self_part = (z % 2 == 0) & (x < 2) & (j == x)
+    self_part = own_zone & (j == 0)
     self_out = own_zone & (x % 2 == j)
-    self_upd = (x % 2) == j
+    self_upd = j == 0
 
     def send(src, dst, ss, rs, device):
         pltpu.make_async_remote_copy(
@@ -75,7 +75,7 @@
         lax.fori_loop(lo, hi, lambda index, carry: (body(index), carry)[1], 0)
 
     def load_known(step):
-        pltpu.make_async_copy(factor.at[step, pl.ds(0, KNOWN)], f_raw.at[step], ld.at[2 + step]).start()
+        pltpu.make_async_copy(factor.at[step, pl.ds(0, KNOWN)], f_raw.at[step], ld.at[16 + step]).start()
 
     def load_inverse(step):
         def one(tile):
@@ -128,16 +128,19 @@
 
         loop(0, GROUPS, one)
 
-    def known_terms(step):
-        wait_local(f_raw.at[step], ld.at[2 + step])
-
+    def split_known(step, first, end):
         def one(group):
             lanes = pl.ds(pl.multiple_of(group * 128, 128), 128)
             high, low = halves(f_raw[step, group])
             f_parts[0:128, lanes] = high
             f_parts[128:256, lanes] = low
 
-        loop(0, KNOWN, one)
+        loop(first, end, one)
+
+    def known_terms(step):
+        if step > 0:
+            wait_local(f_raw.at[step], ld.at[16 + step])
+            split_known(step, 0, KNOWN)
         both = dot(f_parts[...], y_parts[...])
         total = both[0:128, 0:256] + (both[0:128, 256:512] + both[128:256, 0:256] + both[128:256, 256:512])
         known[step] = -(total.T)
@@ -189,18 +192,14 @@
         loop(m + 1, 16, one)
 
     def solve(step, h):
-        def place(tile):
-            lanes = pl.ds(pl.multiple_of(tile * 128, 128), 128)
-            high, low = halves(res[step, h, tile])
-            a_res[h, 0:T, lanes] = high
-            a_res[h, T : 2 * T, lanes] = low
-
         def arrived(tile):
             wait_recv(res.at[step, h, tile], g1_r.at[step, h, tile])
-            place(tile)
-
-        place(m)
+
         loop(0, m, arrived)
+        for tile in range(16):
+            high, low = halves(res[step, h, tile])
+            a_res[h, 0:T, tile * 128 : (tile + 1) * 128] = high
+            a_res[h, T : 2 * T, tile * 128 : (tile + 1) * 128] = low
         both = dot(a_res[h], i_parts[step])
         for t in range(2):
             o = t * 256
@@ -208,14 +207,20 @@
                 both[0:T, o + 128 : o + 256] + both[T : 2 * T, o : o + 128] + both[T : 2 * T, o + 128 : o + 256]
             )
 
+        if step + 1 == STEPS:
+            send_last(h)
+            return
+
         def to(t):
+            column = (z % 2) * 2 + t
+            distance = (x + 4 - column) % 4
             send(
                 part.at[step, h, t], part_in.at[step, h, j], pt_s.at[step, h, t], pt_r.at[step, h, j],
-                at((z % 2) * 2 + t, y, (z + spread) % 4, x % 2),
+                at(column, y, (z + distance % 2) % 4, distance // 2),
             )
 
         for t in range(2):
-            here = self_part & (x == t)
+            here = self_part & (x % 2 == t)
 
             @pl.when(here)
             def _():
@@ -225,10 +230,27 @@
             def _():
                 to(t)
 
+    def send_last(h):
+        for t in range(2):
+            for hop in (2, 1, 3):
+                send(
+                    part.at[STEPS - 1, h, t], last_in.at[h, x, j], ls_s.at[h], ls_r.at[h], at((x + hop) % 4, y, z, t)
+                )
+        last_in[h, x, j] = part[STEPS - 1, h, j]
+        send(part.at[STEPS - 1, h, 1 - j], last_in.at[h, x, j], ls_s.at[h], ls_r.at[h], sibling)
+
+    def collect_last(h):
+        wait_recv(res.at[0, h, pl.ds(0, 7)], ls_r.at[h])
+        for q in range(4):
+            done[STEPS - 1, q * 64 + h * T : q * 64 + (h + 1) * T] = last_in[h, q, 0] + last_in[h, q, 1]
+
+    def drain_last(h):
+        wait_send(res.at[0, h, pl.ds(0, 7)], ls_s.at[h])
+
     def drain_part(step, h):
         for t in range(2):
 
-            @pl.when(jnp.logical_not(self_part & (x == t)))
+            @pl.when(jnp.logical_not(self_part & (x % 2 == t)))
             def _():
                 wait_send(part.at[step, h, t], pt_s.at[step, h, t])
 
@@ -241,16 +263,8 @@
 
         sol[step, h, sol_slot] = part_in[step, h, 0] + part_in[step, h, 1]
         mine = sol.at[step, h, sol_slot]
-        if step + 1 < STEPS:
-
-            def one(index):
-                other = (9 + index) % 15 + 1
-                send(
-                    mine, mine, g2_s.at[step, h], g2_r.at[step, h],
-                    at(x, (y + other // 4) % 4, (z + other % 4) % 4, j),
-                )
-
-            loop(0, 15, one)
+        for dy, dz in PLANE:
+            send(mine, mine, g2_s.at[step, h], g2_r.at[step, h], at(x, (y + dy) % 4, (z + dz) % 4, j))
         rows = pl.ds(pl.multiple_of(q_here * 64 + h * T, T), T)
         for hop in (2, 1, 3):
             send(mine, done.at[step, rows], ot_s.at[step, h], ot_r.at[step], at((x + hop) % 4, y, z_row, x % 2))
@@ -264,8 +278,7 @@
             send(mine, done.at[step, rows], ot_s.at[step, h], ot_r.at[step], at(x, y, z_row, x % 2))
 
     def drain_solution(step, h):
-        if step + 1 < STEPS:
-            wait_send(sol.at[step, h, pl.ds(0, 15)], g2_s.at[step, h])
+        wait_send(sol.at[step, h, pl.ds(0, 15)], g2_s.at[step, h])
 
         @pl.when(self_out)
         def _():
@@ -303,7 +316,7 @@
             return
         for t in range(2):
             for g in range(2):
-                here = (x == 2 * g + j) & (j == t)
+                here = (j == 0) & (g == 0) & (t == 0)
 
                 @pl.when(here)
                 def _():
@@ -313,7 +326,7 @@
                 def _():
                     send(
                         upd.at[step, h, t, g], upd_in.at[step, h, x], up_s.at[step, h], up_r.at[step, h],
-                        at(2 * g + j, y, z, t),
+                        at((x + 2 * j + g) % 4, y, z, t),
                     )
 
     def drain_update(step, h):
@@ -325,15 +338,16 @@
         def _():
             wait_send(upd_in.at[step, h], up_s.at[step, h])
 
+    def collect_done(step):
+        @pl.when(self_out)
+        def _():
+            wait_recv(done.at[step, pl.ds(0, 6 * T)], ot_r.at[step])
+
+        @pl.when(jnp.logical_not(self_out))
+        def _():
+            wait_recv(done.at[step], ot_r.at[step])
+
     def write(step):
-        @pl.when(self_out)
-        def _():
-            wait_recv(done.at[step, pl.ds(0, 6 * T)], ot_r.at[step])
-
-        @pl.when(jnp.logical_not(self_out))
-        def _():
-            wait_recv(done.at[step], ot_r.at[step])
-
         turned[step] = done[step].T
         pltpu.make_async_copy(turned.at[step], out.at[step], wr.at[step]).start()
 
@@ -342,23 +356,33 @@
     def greet(device):
         pl.semaphore_signal(barrier, inc=1, device_id=device, device_id_type=MESH)
 
-    pltpu.make_async_copy(earlier, y_raw, ld.at[0]).start()
-    load_known(0)
-    pltpu.make_async_copy(rhs, b_raw, ld.at[1]).start()
-    load_inverse(0)
+    half = KNOWN // 2
+    for part_of in range(2):
+        groups = pl.ds(part_of * half, half)
+        pltpu.make_async_copy(earlier.at[groups], y_raw.at[groups], ld.at[part_of]).start()
+        pltpu.make_async_copy(factor.at[0, groups], f_raw.at[0, groups], ld.at[2 + part_of]).start()
+    pltpu.make_async_copy(rhs, b_raw, ld.at[16]).start()
 
     def greet_plane(other):
         greet(at(x, (y + other // 4) % 4, (z + other % 4) % 4, j))
 
-    loop(1, 16, greet_plane)
     for hop in range(4):
         for core in range(2):
             if (hop, core) != (0, 0):
                 greet(at((x + hop) % 4, y, z, (j + core) % 2))
             greet(at((x + hop) % 4, y, (z + 1) % 4, (j + core) % 2))
             greet(at((x + hop) % 4, y, (z + 3) % 4, (j + core) % 2))
-    a_res[...] = jnp.zeros_like(a_res)
-    wait_local(y_raw, ld.at[0])
+    loop(1, 16, greet_plane)
+    load_inverse(0)
+    load_update(PAIRS[0])
+    load_known(1)
+
+    def clear(tile):
+        for step in range(STEPS):
+            for h in range(CHAINS):
+                res[step, h, tile] = jnp.zeros((T, 128), F32)
+
+    loop(m + 1, 16, clear)
 
     def split_earlier(group):
         rows = pl.ds(pl.multiple_of(group * 128, 128), 128)
@@ -366,17 +390,20 @@
         y_parts[rows, 0:256] = high
         y_parts[rows, 256:512] = low
 
-    loop(0, KNOWN, split_earlier)
-    wait_local(b_raw, ld.at[1])
+    for part_of in range(2):
+        groups = pl.ds(part_of * half, half)
+        wait_local(y_raw.at[groups], ld.at[part_of])
+        loop(part_of * half, (part_of + 1) * half, split_earlier)
+        wait_local(f_raw.at[0, groups], ld.at[2 + part_of])
+        split_known(0, part_of * half, (part_of + 1) * half)
+    wait_local(b_raw, ld.at[16])
     known_terms(0)
     pl.semaphore_wait(barrier, 15 + 7 + 16)
     send_known(0)
     share_inverse(0)
-    load_update(PAIRS[0])
-    load_known(1)
     share_update(PAIRS[0])
-    load_known(2)
-    load_known(3)
+    for step in range(2, STEPS):
+        load_known(step)
     collect_known(0)
     for h in range(CHAINS):
         send_residual(0, h)
@@ -389,67 +416,69 @@
     for step in range(STEPS):
         for h in range(CHAINS):
             solve(step, h)
+        if step + 1 == STEPS:
+            break
         if step == 0:
             prepare_update(PAIRS[0])
             known_terms(1)
             send_known(1)
-        elif step + 1 < STEPS:
-            for h in range(CHAINS):
-                drain_residual(step - 1, h)
-                drain_solution(step - 1, h)
-                drain_part(step - 1, h)
         for h in range(CHAINS):
             send_solution(step, h)
-        if step + 1 == STEPS:
-            break
         if step == 0:
             share_inverse(1)
             for pair in PAIRS[1:]:
                 share_update(pair)
             known_terms(2)
             send_known(2)
-            known_terms(3)
-            send_known(3)
             collect_known(1)
-            prepare_update((2, 0))
-            prepare_update((3, 0))
         elif step == 1:
             share_inverse(3)
             prepare_inverse(2)
         for h in range(CHAINS):
+            drain_part(step, h)
+        for h in range(CHAINS):
             gather_solution(step, h)
             update(step, step + 1, h)
+        if step == 0:
+            prepare_update((2, 0))
+            prepare_update((3, 0))
         for later_step in range(step + 2, STEPS):
             for h in range(CHAINS):
                 update(step, later_step, h)
         if step == 0:
             share_inverse(2)
-            collect_known(2)
-            collect_known(3)
         for h in range(CHAINS):
             send_residual(step + 1, h)
         if step == 0:
             prepare_inverse(1)
+            known_terms(3)
+            send_known(3)
+            collect_known(2)
             prepare_update((2, 1))
             prepare_update((3, 1))
         elif step == 1:
             prepare_inverse(3)
             prepare_update((3, 2))
+            collect_known(3)
+        collect_done(step)
         write(step)
         for h in range(CHAINS):
             drain_update(step, h)
+            drain_residual(step, h)
+            drain_solution(step, h)
 
     for step in range(STEPS):
         wait_send(known.at[step, pl.ds(0, 192)], kn_s.at[step])
         wait_send(i_raw.at[step, j], sib_s.at[step])
     for slot in range(len(PAIRS)):
         wait_send(u_raw.at[slot, j], sib_s.at[4 + slot])
-    for step in range(STEPS - 2, STEPS):
-        for h in range(CHAINS):
-            drain_residual(step, h)
-            drain_part(step, h)
-            drain_solution(step, h)
+    for h in range(CHAINS):
+        drain_residual(STEPS - 1, h)
+    for h in range(CHAINS):
+        collect_last(h)
     write(STEPS - 1)
+    for h in range(CHAINS):
+        drain_last(h)
     for step in range(STEPS):
         wait_local(turned.at[step], wr.at[step])
 
@@ -486,9 +515,10 @@
             vmem((2, CHAINS, 2, 2 * T, 128), F32),
             vmem((STEPS, 256, 128), F32),
             vmem((STEPS, 128, 256), F32),
+            vmem((CHAINS, 4, 2, T, 128), F32),
             vmem((CHAINS, 2 * T, 2048), BF16),
             vmem((CHAINS, 4 * T, 1024), BF16),
-            dma((16,)),
+            dma((20,)),
             dma((10,)),
             dma((10,)),
             dma((STEPS,)),
@@ -503,6 +533,8 @@
             dma((STEPS,)),
             dma((STEPS, CHAINS)),
             dma((STEPS, CHAINS)),
+            dma((CHAINS,)),
+            dma((CHAINS,)),
             dma((STEPS,)),
         ],
         compiler_params=pltpu.CompilerParams(

time: 101 us -> 96 us (0.950); the launches traced: 98.7 us -> 95.8 us
  Pallas kernels: 96.8 us -> 93.9 us
    pallas_call x1, Pallas kernels: 96.8 us -> 93.9 us  [per_device(): pl.pallas_call(kernel, out_shape=jax.ShapeDtypeStruct(rhs.shape, F32), in...]
where the time goes in v3:
time: 96 us; the launch traced here: 95.8 us
  Pallas kernels  93.9 us (98%)
  local copies, waits for them, and re-layouts  1.87 us (2%)
    pallas_call x1, Pallas kernels, per_device(): pl.pallas_call(kernel, out_shape=jax.ShapeDtypeStruct(rhs.shape, F32), in...  93.9 us

profile of v3, /device:TPU:19, one launch (start us, length us, event | category | flops | bytes accessed | tf_op | source)
XLA Modules:
  0.0 95.8 jit_solution(12447808395160917411)
XLA Ops:
  0.0 93.9 %substitution.1 = f32[4,128,256]{2,1,0:T(8,128)} custom-call(f32[4,52,128,128]{3,2,1,0:T(8,128)} %bitcast.1, f32[20,128,256]{2,1,0:T(8,128)} %earlier.1, f32[4,128,256]{2,1,0:T(8,128)} %rhs.1, f32[4,128,4096]{2,1,0:T(8,128)} %inverse.1), custom_call_target="tpu_custom_call" | custom-call | flops 6000000000 | bytes 20000000 | tf_op jit(solution)/shard_map/substitution/pallas_call | solution.py:490
  93.9 1.9 %copy.6 = f32[4,128,256]{2,1,0:T(8,128)} copy(f32[4,128,256]{2,1,0:T(8,128)} %substitution.1) | data formatting | bytes 1048576

commit v4 on v3

--- a/solution.py
+++ b/solution.py
@@ -138,10 +138,11 @@
         loop(first, end, one)
 
     def known_terms(step):
-        if step > 0:
-            wait_local(f_raw.at[step], ld.at[16 + step])
-            split_known(step, 0, KNOWN)
-        both = dot(f_parts[...], y_parts[...])
+        wait_local(f_raw.at[step], ld.at[16 + step])
+        split_known(step, 0, KNOWN)
+        finish_known(step, dot(f_parts[...], y_parts[...]))
+
+    def finish_known(step, both):
         total = both[0:128, 0:256] + (both[0:128, 256:512] + both[128:256, 0:256] + both[128:256, 256:512])
         known[step] = -(total.T)
         b_turn[...] = b_raw[step].T
@@ -265,6 +266,9 @@
         mine = sol.at[step, h, sol_slot]
         for dy, dz in PLANE:
             send(mine, mine, g2_s.at[step, h], g2_r.at[step, h], at(x, (y + dy) % 4, (z + dz) % 4, j))
+
+    def send_done(step, h):
+        mine = sol.at[step, h, sol_slot]
         rows = pl.ds(pl.multiple_of(q_here * 64 + h * T, T), T)
         for hop in (2, 1, 3):
             send(mine, done.at[step, rows], ot_s.at[step, h], ot_r.at[step], at((x + hop) % 4, y, z_row, x % 2))
@@ -390,81 +394,85 @@
         y_parts[rows, 0:256] = high
         y_parts[rows, 256:512] = low
 
+    both = None
     for part_of in range(2):
         groups = pl.ds(part_of * half, half)
         wait_local(y_raw.at[groups], ld.at[part_of])
         loop(part_of * half, (part_of + 1) * half, split_earlier)
         wait_local(f_raw.at[0, groups], ld.at[2 + part_of])
         split_known(0, part_of * half, (part_of + 1) * half)
+        span = slice(part_of * half * 128, (part_of + 1) * half * 128)
+        product = dot(f_parts[:, span], y_parts[span, :])
+        both = product if both is None else both + product
     wait_local(b_raw, ld.at[16])
-    known_terms(0)
+    finish_known(0, both)
     pl.semaphore_wait(barrier, 15 + 7 + 16)
     send_known(0)
     share_inverse(0)
     share_update(PAIRS[0])
     for step in range(2, STEPS):
         load_known(step)
+    load_inverse(1)
     collect_known(0)
     for h in range(CHAINS):
         send_residual(0, h)
     prepare_inverse(0)
-    for step in range(1, STEPS):
+    for step in range(2, STEPS):
         load_inverse(step)
     for pair in PAIRS[1:]:
         load_update(pair)
+    known_terms(1)
+    send_known(1)
+    prepare_update((1, 0))
 
     for step in range(STEPS):
         for h in range(CHAINS):
             solve(step, h)
         if step + 1 == STEPS:
             break
-        if step == 0:
-            prepare_update(PAIRS[0])
-            known_terms(1)
-            send_known(1)
         for h in range(CHAINS):
             send_solution(step, h)
+        for h in range(CHAINS):
+            send_done(step, h)
         if step == 0:
             share_inverse(1)
-            for pair in PAIRS[1:]:
-                share_update(pair)
             known_terms(2)
             send_known(2)
             collect_known(1)
+            for pair in PAIRS[1:]:
+                share_update(pair)
         elif step == 1:
             share_inverse(3)
-            prepare_inverse(2)
-        for h in range(CHAINS):
-            drain_part(step, h)
-        for h in range(CHAINS):
-            gather_solution(step, h)
-            update(step, step + 1, h)
-        if step == 0:
-            prepare_update((2, 0))
-            prepare_update((3, 0))
-        for later_step in range(step + 2, STEPS):
-            for h in range(CHAINS):
-                update(step, later_step, h)
-        if step == 0:
-            share_inverse(2)
-        for h in range(CHAINS):
-            send_residual(step + 1, h)
-        if step == 0:
-            prepare_inverse(1)
             known_terms(3)
             send_known(3)
             collect_known(2)
             prepare_update((2, 1))
-            prepare_update((3, 1))
-        elif step == 1:
+        elif step == 2:
             prepare_inverse(3)
             prepare_update((3, 2))
             collect_known(3)
+        for h in range(CHAINS):
+            gather_solution(step, h)
+            update(step, step + 1, h)
+        for h in range(CHAINS):
+            send_residual(step + 1, h)
+        if step == 0:
+            prepare_inverse(1)
+            share_inverse(2)
+            prepare_update((2, 0))
+            prepare_update((3, 0))
+        elif step == 1:
+            prepare_inverse(2)
+            prepare_update((3, 1))
+        for later_step in range(step + 2, STEPS):
+            for h in range(CHAINS):
+                update(step, later_step, h)
         collect_done(step)
         write(step)
         for h in range(CHAINS):
             drain_update(step, h)
             drain_residual(step, h)
+            drain_part(step, h)
             drain_solution(step, h)
 
     for step in range(STEPS):

time: 96 us -> 94.9 us (0.989)
  Pallas kernels: 93.9 us -> 92.9 us
    pallas_call x1, Pallas kernels: 93.9 us -> 92.9 us  [per_device(): pl.pallas_call(kernel, out_shape=jax.ShapeDtypeStruct(rhs.shape, F32), in...]
where the time goes in v4:
time: 94.9 us; the launch traced here: 94.8 us
  Pallas kernels  92.9 us (98%)
  local copies, waits for them, and re-layouts  1.87 us (2%)
    pallas_call x1, Pallas kernels, per_device(): pl.pallas_call(kernel, out_shape=jax.ShapeDtypeStruct(rhs.shape, F32), in...  92.9 us

profile of v4, /device:TPU:19, one launch (start us, length us, event | category | flops | bytes accessed | tf_op | source)
XLA Modules:
  0.0 94.8 jit_solution(1847621725186514476)
XLA Ops:
  0.0 92.9 %substitution.1 = f32[4,128,256]{2,1,0:T(8,128)} custom-call(f32[4,52,128,128]{3,2,1,0:T(8,128)} %bitcast.1, f32[20,128,256]{2,1,0:T(8,128)} %earlier.1, f32[4,128,256]{2,1,0:T(8,128)} %rhs.1, f32[4,128,4096]{2,1,0:T(8,128)} %inverse.1), custom_call_target="tpu_custom_call" | custom-call | flops 6000000000 | bytes 20000000 | tf_op jit(solution)/shard_map/substitution/pallas_call | solution.py:498
  92.9 1.9 %copy.6 = f32[4,128,256]{2,1,0:T(8,128)} copy(f32[4,128,256]{2,1,0:T(8,128)} %substitution.1) | data formatting | bytes 1048576

commit v5 on v4

--- a/solution.py
+++ b/solution.py
@@ -32,8 +32,8 @@
 def kernel(
     factor, earlier, rhs, inverse, out,
     y_raw, y_parts, f_raw, f_parts, u_raw, u_parts, i_raw, i_parts, b_raw, b_turn,
-    known, known_in, start, res, sol, upd_in, part_in, part, upd, later, done, turned, last_in, a_res, a_sol,
-    ld, sib_s, sib_r, kn_s, kn_r, g1_s, g1_r, pt_s, pt_r, g2_s, g2_r, ot_s, ot_r, up_s, up_r, ls_s, ls_r, wr,
+    known, known_in, start, res, sol, upd_in, part_in, part, upd, later, done, last_in, a_res, a_sol,
+    ld, sib_s, sib_r, kn_s, kn_r, g1_s, g1_r, pt_s, pt_r, g2_s, g2_r, ot_s, ot_r, up_s, up_r, ls_s, ls_r,
 ):
     row = lax.axis_index("row")
     x = lax.axis_index("col")
@@ -178,7 +178,8 @@
                 upd_in[step - 1, h, 0] + upd_in[step - 1, h, 1] + upd_in[step - 1, h, 2] + upd_in[step - 1, h, 3]
             )
 
-        def one(other):
+        def one(index):
+            other = 16 + m - index
             send(
                 res.at[step, h, m], res.at[step, h, m], g1_s.at[step, h, other], g1_r.at[step, h, m],
                 at(x, other // 4, other % 4, j),
@@ -352,8 +353,7 @@
             wait_recv(done.at[step], ot_r.at[step])
 
     def write(step):
-        turned[step] = done[step].T
-        pltpu.make_async_copy(turned.at[step], out.at[step], wr.at[step]).start()
+        out[step] = done[step].T
 
     barrier = pltpu.get_barrier_semaphore()
 
@@ -487,8 +487,6 @@
     write(STEPS - 1)
     for h in range(CHAINS):
         drain_last(h)
-    for step in range(STEPS):
-        wait_local(turned.at[step], wr.at[step])
 
 
 def per_device(factor, earlier, rhs, inverse):
@@ -497,9 +495,9 @@
     updates = len(PAIRS)
     return pl.pallas_call(
         kernel,
-        out_shape=jax.ShapeDtypeStruct(rhs.shape, F32),
+        out_shape=pltpu.VMEM(rhs.shape, F32),
         in_specs=[pl.BlockSpec(memory_space=pl.ANY)] * 4,
-        out_specs=pl.BlockSpec(memory_space=pl.ANY),
+        out_specs=pl.BlockSpec(memory_space=pltpu.VMEM),
         scratch_shapes=[
             vmem((KNOWN, 128, 256), F32),
             vmem((KNOWN * 128, 512), BF16),
@@ -522,7 +520,6 @@
             vmem((STEPS - 1, CHAINS, 2, 2, T, 128), F32),
             vmem((2, CHAINS, 2, 2 * T, 128), F32),
             vmem((STEPS, 256, 128), F32),
-            vmem((STEPS, 128, 256), F32),
             vmem((CHAINS, 4, 2, T, 128), F32),
             vmem((CHAINS, 2 * T, 2048), BF16),
             vmem((CHAINS, 4 * T, 1024), BF16),
@@ -543,7 +540,6 @@
             dma((STEPS, CHAINS)),
             dma((CHAINS,)),
             dma((CHAINS,)),
-            dma((STEPS,)),
         ],
         compiler_params=pltpu.CompilerParams(
             collective_id=0, has_side_effects=True, vmem_limit_bytes=60 * 1024 * 1024

time: 94.9 us -> 93 us (0.980)
  Pallas kernels: 92.9 us -> 91.1 us
  local copies, waits for them, and re-layouts: 1.87 us -> 0.8 us
    pallas_call x1, Pallas kernels: 92.9 us -> 91.1 us  [per_device(): pl.pallas_call(kernel, out_shape=pltpu.VMEM(rhs.shape, F32), in_specs=[pl...]
    unnamed x1, local copies, waits for them, and re-layouts: 1.87 us -> 0.8 us
where the time goes in v5:
time: 93 us; the launch traced here: 91.9 us
  Pallas kernels  91.1 us (98%)
    pallas_call x1, Pallas kernels, per_device(): pl.pallas_call(kernel, out_shape=pltpu.VMEM(rhs.shape, F32), in_specs=[pl...  91.1 us

profile of v5, /device:TPU:19, one launch (start us, length us, event | category | flops | bytes accessed | tf_op | source)
XLA Modules:
  0.0 91.9 jit_solution(6697829785007521659)
XLA Ops:
  0.0 91.1 %substitution.1 = f32[4,128,256]{2,1,0:T(8,128)S(1)} custom-call(f32[4,52,128,128]{3,2,1,0:T(8,128)} %bitcast.1, f32[20,128,256]{2,1,0:T(8,128)} %earlier.1, f32[4,128,256]{2,1,0:T(8,128)} %rhs.1, f32[4,128,4096]{2,1,0:T(8,128)} %inverse.1), custom_call_target="tpu_custom_call" | custom-call | flops 6000000000 | bytes 20000000 | tf_op jit(solution)/shard_map/substitution/pallas_call | solution.py:496
  91.1 0.8 copy.6

commit v6 on v5

--- a/solution.py
+++ b/solution.py
@@ -180,9 +180,10 @@
 
         def one(index):
             other = 16 + m - index
+            y_to = other // 4
             send(
-                res.at[step, h, m], res.at[step, h, m], g1_s.at[step, h, other], g1_r.at[step, h, m],
-                at(x, other // 4, other % 4, j),
+                res.at[step, h, m], res.at[step, h, m], g1_s.at[step, h, other],
+                g1_r.at[step, h, jnp.where(y_to == y, 4 + z, y)], at(x, y_to, other % 4, j),
             )
 
         loop(m + 1, 16, one)
@@ -194,15 +195,27 @@
         loop(m + 1, 16, one)
 
     def solve(step, h):
-        def arrived(tile):
-            wait_recv(res.at[step, h, tile], g1_r.at[step, h, tile])
-
-        loop(0, m, arrived)
-        for tile in range(16):
-            high, low = halves(res[step, h, tile])
-            a_res[h, 0:T, tile * 128 : (tile + 1) * 128] = high
-            a_res[h, T : 2 * T, tile * 128 : (tile + 1) * 128] = low
-        both = dot(a_res[h], i_parts[step])
+        def arrived(other):
+            wait_recv(res.at[step, h, y * 4 + other], g1_r.at[step, h, 4 + other])
+
+        both = None
+        for band in (3, 0, 2, 1):
+
+            @pl.when(y == band)
+            def _():
+                loop(0, z, arrived)
+
+            @pl.when(y > band)
+            def _():
+                wait_recv(res.at[step, h, pl.ds(band * 4, 4)], g1_r.at[step, h, band])
+
+            for tile in range(band * 4, band * 4 + 4):
+                high, low = halves(res[step, h, tile])
+                a_res[h, 0:T, tile * 128 : (tile + 1) * 128] = high
+                a_res[h, T : 2 * T, tile * 128 : (tile + 1) * 128] = low
+            span = slice(band * 512, (band + 1) * 512)
+            product = dot(a_res[h, :, span], i_parts[step, span, :])
+            both = product if both is None else both + product
         for t in range(2):
             o = t * 256
             part[step, h, t] = both[0:T, o : o + 128] + (
@@ -266,7 +279,7 @@
         sol[step, h, sol_slot] = part_in[step, h, 0] + part_in[step, h, 1]
         mine = sol.at[step, h, sol_slot]
         for dy, dz in PLANE:
-            send(mine, mine, g2_s.at[step, h], g2_r.at[step, h], at(x, (y + dy) % 4, (z + dz) % 4, j))
+            send(mine, mine, g2_s.at[step, h], g2_r.at[step, h, dy], at(x, (y + dy) % 4, (z + dz) % 4, j))
 
     def send_done(step, h):
         mine = sol.at[step, h, sol_slot]
@@ -293,16 +306,28 @@
         def _():
             wait_send(sol.at[step, h, pl.ds(0, 4)], ot_s.at[step, h])
 
-    def gather_solution(step, h):
-        wait_recv(sol.at[step, h, pl.ds(0, 15)], g2_r.at[step, h])
-        for g in range(2):
-            for b in range(GROUPS):
-                high, low = halves(sol[step, h, g * 8 + b])
-                a_sol[h, g * T : (g + 1) * T, b * 128 : (b + 1) * 128] = high
-                a_sol[h, 2 * T + g * T : 2 * T + (g + 1) * T, b * 128 : (b + 1) * 128] = low
+    def gather_update(step, h):
+        both = None
+        for dy in (0, 1, 3, 2):
+            wait_recv(sol.at[step, h, pl.ds(0, 4 if dy else 3)], g2_r.at[step, h, dy])
+            source = (y + 4 - dy) % 4
+            span = pl.ds(pl.multiple_of(source * 256, 256), 256)
+            parts = []
+            for g in range(2):
+                parts.append([halves(sol[step, h, g * 8 + source * 2 + b]) for b in range(2)])
+            left = jnp.concatenate(
+                [jnp.concatenate([parts[g][b][side] for b in range(2)], axis=1) for side in range(2) for g in range(2)],
+                axis=0,
+            )
+            a_sol[h, :, span] = left
+            product = dot(left, u_parts[SLOT[step + 1, step], span, :])
+            both = product if both is None else both + product
+        finish_update(step, step + 1, h, both)
 
     def update(step, later_step, h):
-        both = dot(a_sol[h], u_parts[SLOT[later_step, step]])
+        finish_update(step, later_step, h, dot(a_sol[h], u_parts[SLOT[later_step, step]]))
+
+    def finish_update(step, later_step, h, both):
         for t in range(2):
             o = t * 256
             total = both[0 : 2 * T, o : o + 128] + (
@@ -452,8 +477,7 @@
             prepare_update((3, 2))
             collect_known(3)
         for h in range(CHAINS):
-            gather_solution(step, h)
-            update(step, step + 1, h)
+            gather_update(step, h)
         for h in range(CHAINS):
             send_residual(step + 1, h)
         if step == 0:
@@ -529,11 +553,11 @@
             dma((STEPS,)),
             dma((STEPS,)),
             dma((STEPS, CHAINS, 16)),
-            dma((STEPS, CHAINS, 16)),
+            dma((STEPS, CHAINS, 8)),
             dma((STEPS, CHAINS, 2)),
             dma((STEPS, CHAINS, 2)),
             dma((STEPS, CHAINS)),
-            dma((STEPS, CHAINS)),
+            dma((STEPS, CHAINS, 4)),
             dma((STEPS, CHAINS)),
             dma((STEPS,)),
             dma((STEPS, CHAINS)),

time: 93 us -> 92.6 us (level)
  no operation moved by 1% of the time
where the time goes in v6:
time: 92.6 us; the launch traced here: 91.5 us
  Pallas kernels  90.7 us (98%)
    pallas_call x1, Pallas kernels, per_device(): pl.pallas_call(kernel, out_shape=pltpu.VMEM(rhs.shape, F32), in_specs=[pl...  90.7 us

profile of v6, /device:TPU:19, one launch (start us, length us, event | category | flops | bytes accessed | tf_op | source)
XLA Modules:
  0.0 91.5 jit_solution(7867383140575272780)
XLA Ops:
  0.0 90.7 %substitution.1 = f32[4,128,256]{2,1,0:T(8,128)S(1)} custom-call(f32[4,52,128,128]{3,2,1,0:T(8,128)} %bitcast.1, f32[20,128,256]{2,1,0:T(8,128)} %earlier.1, f32[4,128,256]{2,1,0:T(8,128)} %rhs.1, f32[4,128,4096]{2,1,0:T(8,128)} %inverse.1), custom_call_target="tpu_custom_call" | custom-call | flops 6000000000 | bytes 20000000 | tf_op jit(solution)/shard_map/substitution/pallas_call | solution.py:520
  90.7 0.8 copy.6

commit v7 on v6

--- a/solution.py
+++ b/solution.py
@@ -178,15 +178,18 @@
                 upd_in[step - 1, h, 0] + upd_in[step - 1, h, 1] + upd_in[step - 1, h, 2] + upd_in[step - 1, h, 3]
             )
 
-        def one(index):
-            other = 16 + m - index
-            y_to = other // 4
+        def one(y_to, z_to, sem):
             send(
-                res.at[step, h, m], res.at[step, h, m], g1_s.at[step, h, other],
-                g1_r.at[step, h, jnp.where(y_to == y, 4 + z, y)], at(x, y_to, other % 4, j),
+                res.at[step, h, m], res.at[step, h, m], g1_s.at[step, h, y_to * 4 + z_to], g1_r.at[step, h, sem],
+                at(x, y_to, z_to, j),
             )
 
-        loop(m + 1, 16, one)
+        def row_of_chips(index):
+            for dz in (2, 1, 3, 0):
+                one(4 + y - index, (z + dz) % 4, y)
+
+        loop(y + 1, 4, row_of_chips)
+        loop(z + 1, 4, lambda index: one(y, 4 + z - index, 4 + z))
 
     def drain_residual(step, h):
         def one(other):

time: 92.6 us -> 91.8 us (level)
  Pallas kernels: 90.7 us -> 89.4 us
    pallas_call x1, Pallas kernels: 90.7 us -> 89.4 us  [per_device(): pl.pallas_call(kernel, out_shape=pltpu.VMEM(rhs.shape, F32), in_specs=[pl...]
where the time goes in v7:
time: 91.8 us; the launch traced here: 90.2 us
  Pallas kernels  89.4 us (97%)
    pallas_call x1, Pallas kernels, per_device(): pl.pallas_call(kernel, out_shape=pltpu.VMEM(rhs.shape, F32), in_specs=[pl...  89.4 us

profile of v7, /device:TPU:19, one launch (start us, length us, event | category | flops | bytes accessed | tf_op | source)
XLA Modules:
  0.0 90.2 jit_solution(750379012534825177)
XLA Ops:
  0.0 89.4 %substitution.1 = f32[4,128,256]{2,1,0:T(8,128)S(1)} custom-call(f32[4,52,128,128]{3,2,1,0:T(8,128)} %bitcast.1, f32[20,128,256]{2,1,0:T(8,128)} %earlier.1, f32[4,128,256]{2,1,0:T(8,128)} %rhs.1, f32[4,128,4096]{2,1,0:T(8,128)} %inverse.1), custom_call_target="tpu_custom_call" | custom-call | flops 6000000000 | bytes 20000000 | tf_op jit(solution)/shard_map/substitution/pallas_call | solution.py:523
  89.4 0.8 copy.6
